TPU v7x, 512 devices: a whole 4x4x16 slice. The times are simulated.
512 devices in a mesh: seq: 64 (over z, x), kvh: 8 (over y, core).
Axes of the slice: x: 4, y: 4, z: 16, core: 2. Of those that a mesh axis runs over, the one named last changes fastest.
Arguments:
- hidden: bfloat16 [16, 8192], P(None, 'seq'), may hold values from -4 to 4
- filter_query: bfloat16 [16, 8192], P(None, 'kvh'), as said below
- new_entry: bfloat16 [16, 2048], P(None, 'kvh'), may hold values from -6 to 6
- filter_cache: bfloat16 [16, 8192, 2048], P(None, 'seq', 'kvh'), as said below
- out_weight: bfloat16 [8192, 8192], P('kvh', 'seq'), may hold values from -0.0625 to 0.0625
- next_gain: float32 [8192], P('seq'), may hold values from 0.5 to 2
- next_weight: bfloat16 [8192, 8, 1280], P('seq', 'kvh'), may hold values from -0.0625 to 0.0625
- next_cache: bfloat16 [16, 8192, 2048], P(None, 'seq', 'kvh'), as said below
- lengths: int32 [16], replicated, may hold values from 4096 to 8192, as said below
- selected: int32 [16, 2048], replicated, may hold values from 0 to 8191, as said below
Outputs:
- filter_out: bfloat16 [16, 8192], P(None, 'kvh')
- next_hidden: bfloat16 [16, 8192], P(None, 'seq')
- compact_cache: bfloat16 [64, 512, 2048], P('seq', None, 'kvh')
- select_out: bfloat16 [16, 8192], P(None, 'kvh')
Inputs may be any that keep to these rules, and one draw needn't show every extreme that they name: The new token of request r stands at position lengths[r]; some request has exactly 8192. `selected`: each request's 2048 positions are distinct, ascending and below lengths[r]. For each request at most 64 of them lie in any aligned block of 128 positions, and in every draw some request has exactly 64 in one block. `filter_query`: rotated queries of order 2.5. `filter_cache`: cached keys and values of order one. `next_cache`: cached keys and values of order one.
All inputs are finite; a program needn't handle non-finite values.
Results may differ from a plain program's by a relative error of at most 0.038.
Values may be sent and summed in bfloat16 or wider, within the bound.
A program may use at most 64 MiB of HBM per device.

v0:
```python
import math

import jax
import jax.numpy as jnp
from jax import lax
from jax.sharding import PartitionSpec as P

D = 8192
HD = 128
SEL = 2048


NEG_FILL = -1e30
ROPE_BASE = 500000.0
EPSILON = 1e-05


def joined(part, axis, combine):
    gathered = jax.tree.map(lambda a: lax.all_gather(a, axis), part)

    def take(source):
        return jax.tree.map(lambda a: lax.dynamic_index_in_dim(a, source, 0, False), gathered)

    return lax.fori_loop(
        1, lax.axis_size(axis), lambda source, state: combine(state, take(source)), take(0)
    )


def rotary(values, lengths):
    half_dim = values.shape[-1] // 2
    inverse = 1.0 / ROPE_BASE ** (jnp.arange(half_dim, dtype=jnp.float32) * 2.0 / values.shape[-1])
    angles = lengths.astype(jnp.float32)[:, None] * inverse[None, :]
    view_shape = (values.shape[0],) + (1,) * (values.ndim - 2) + (half_dim,)
    cosine = jnp.cos(angles).reshape(view_shape)
    sine_part = jnp.sin(angles).reshape(view_shape)
    first_half = values[..., :half_dim]
    second_half = values[..., half_dim:]
    return jnp.concatenate(
        [
            first_half * cosine - second_half * sine_part,
            second_half * cosine + first_half * sine_part,
        ],
        axis=-1,
    )


def split_cache(cache_rows, heads_kv):
    shaped = cache_rows.reshape(cache_rows.shape[0], cache_rows.shape[1], heads_kv, 2, HD)
    return (shaped[:, :, :, 0], shaped[:, :, :, 1])


def scores_of(query, keys, row_alive):
    scores = jnp.einsum(
        "rhgd,rnhd->rhgn", query, keys, preferred_element_type=jnp.float32
    ) / math.sqrt(HD)
    return jnp.where(row_alive[:, None, None, :], scores, NEG_FILL)


def weigh_values(scores, peak_score, values, row_alive):
    weights = jnp.where(row_alive[:, None, None, :], jnp.exp(scores - peak_score[..., None]), 0.0)
    weight_sum = jnp.sum(weights, axis=-1)
    weighted = jnp.einsum(
        "rhgn,rnhd->rhgd", weights.astype(jnp.bfloat16), values, preferred_element_type=jnp.float32
    )
    return (weight_sum, weighted)


def partial_softmax(query, keys, values, row_alive):
    scores = scores_of(query, keys, row_alive)
    peak_score = jnp.max(scores, axis=-1)
    weight_sum, weighted = weigh_values(scores, peak_score, values, row_alive)
    return (peak_score, weight_sum, weighted)


def combine(left, right):
    new_peak = jnp.maximum(left[0], right[0])
    left_fade = jnp.exp(left[0] - new_peak)
    right_fade = jnp.exp(right[0] - new_peak)
    weight_sum = left[1] * left_fade + right[1] * right_fade
    weighted = left[2] * left_fade[..., None] + right[2] * right_fade[..., None]
    return (new_peak, weight_sum, weighted)


def finish(peak_score, weight_sum, weighted, query, new_key, new_value):
    own_score = jnp.einsum(
        "rhgd,rhd->rhg", query, new_key, preferred_element_type=jnp.float32
    ) / math.sqrt(HD)
    new_peak = jnp.maximum(peak_score, own_score)
    rescale = jnp.exp(peak_score - new_peak)
    own_weight = jnp.exp(own_score - new_peak)
    weight_sum = weight_sum * rescale + own_weight
    own_rounded = own_weight.astype(jnp.bfloat16).astype(jnp.float32)
    weighted = (
        weighted * rescale[..., None]
        + own_rounded[..., None] * new_value.astype(jnp.float32)[:, :, None, :]
    )
    result = (weighted / weight_sum[..., None]).astype(jnp.bfloat16)
    return result.reshape(result.shape[0], -1)


def per_device(
    hidden,
    filter_query,
    new_entry,
    filter_cache,
    out_weight,
    next_gain,
    next_weight,
    next_cache,
    lengths,
    selected,
):
    seq_count = lax.axis_size("seq")
    my_index = lax.axis_index("seq")
    requests = hidden.shape[0]
    rows_here = filter_cache.shape[1]
    heads_kv = new_entry.shape[1] // (2 * HD)
    per_group = filter_query.shape[1] // (heads_kv * HD)
    row_base = my_index * rows_here
    request_ids = jnp.arange(requests, dtype=jnp.int32)
    first_query = filter_query.reshape(requests, heads_kv, per_group, HD)
    first_fresh = new_entry.reshape(requests, heads_kv, 2, HD)
    positions = row_base + jnp.arange(rows_here, dtype=jnp.int32)
    row_alive = positions[None, :] < lengths[:, None]
    first_keys, first_values = split_cache(filter_cache, heads_kv)
    peak_score, weight_sum, weighted = partial_softmax(
        first_query, first_keys, first_values, row_alive
    )
    peak_score, weight_sum, weighted = joined((peak_score, weight_sum, weighted), "seq", combine)
    filter_out = finish(
        peak_score, weight_sum, weighted, first_query, first_fresh[:, :, 0], first_fresh[:, :, 1]
    )
    mixed_out = lax.psum(jnp.dot(filter_out, out_weight, preferred_element_type=jnp.float32), "kvh")
    next_hidden = (hidden.astype(jnp.float32) + mixed_out).astype(jnp.bfloat16)
    widened = next_hidden.astype(jnp.float32)
    scaled = (widened * next_gain[None, :]).astype(jnp.bfloat16)
    projected = jnp.dot(
        scaled, next_weight.reshape(next_weight.shape[0], -1), preferred_element_type=jnp.float32
    )
    projected, squares = lax.psum((projected, jnp.sum(widened * widened, axis=1)), "seq")
    projected = projected * lax.rsqrt(squares / D + EPSILON)[:, None]
    projected = projected.reshape(requests, heads_kv, per_group + 2, HD)
    next_query = rotary(projected[:, :, :per_group], lengths).astype(jnp.bfloat16)
    next_key = rotary(projected[:, :, per_group], lengths).astype(jnp.bfloat16)
    next_value = projected[:, :, per_group + 1].astype(jnp.bfloat16)
    shard_cap = 2 * SEL // seq_count
    owners = seq_count // requests
    pair_slots = shard_cap // owners
    owner_rows = SEL // owners
    flat_rows = next_cache.reshape(requests * rows_here, -1)
    flat_selected = selected.reshape(-1)
    before = jnp.sum((selected < row_base).astype(jnp.int32), axis=1)
    inside = jnp.sum(
        ((selected >= row_base) & (selected < row_base + rows_here)).astype(jnp.int32), axis=1
    )
    first_pos = jnp.repeat(before, owners)
    run_count = jnp.repeat(inside, owners)
    owner_req = jnp.repeat(request_ids, owners)
    owner_part = jnp.tile(jnp.arange(owners, dtype=jnp.int32), requests)
    start_slot = first_pos + (owner_part - first_pos) % owners
    entry_pos = start_slot[:, None] + owners * jnp.arange(pair_slots, dtype=jnp.int32)[None, :]
    usable = entry_pos < (first_pos + run_count)[:, None]
    picked = jnp.take(flat_selected, owner_req[:, None] * SEL + jnp.minimum(entry_pos, SEL - 1))
    local_row = jnp.clip(picked - row_base, 0, rows_here - 1)
    taken = jnp.take(flat_rows, (owner_req[:, None] * rows_here + local_row).reshape(-1), axis=0)
    taken = taken.reshape(seq_count, pair_slots, -1)
    outgoing = jnp.where(usable[:, :, None], taken, jnp.zeros((), jnp.bfloat16))
    incoming = lax.all_to_all(outgoing, "seq", split_axis=0, concat_axis=0, tiled=True)
    mine_req = my_index // owners
    mine_part = my_index % owners
    own_selected = lax.dynamic_index_in_dim(selected, mine_req, axis=0, keepdims=False)
    source_ids = jnp.arange(seq_count, dtype=jnp.int32)
    starts = jnp.sum(
        (own_selected[None, :] < (source_ids * rows_here)[:, None]).astype(jnp.int32), axis=1
    )
    first_slot = starts + (mine_part - starts) % owners
    wanted = mine_part + owners * jnp.arange(owner_rows, dtype=jnp.int32)
    source = jnp.take(own_selected, wanted) // rows_here
    first_at = jnp.sum(
        jnp.where(source[:, None] == source_ids[None, :], first_slot[None, :], 0), axis=1
    )
    slot_index = (wanted - first_at) // owners
    compact = jnp.take(
        incoming.reshape(seq_count * pair_slots, -1), source * pair_slots + slot_index, axis=0
    )
    compact_cache = compact[None]
    owner_keys, owner_values = split_cache(compact_cache, heads_kv)
    query_mine = lax.dynamic_slice_in_dim(next_query, mine_req, 1, axis=0)
    every_row = jnp.arange(owner_rows, dtype=jnp.int32)[None, :] >= 0
    peak_one, sum_one, weighted_one = partial_softmax(
        query_mine, owner_keys, owner_values, every_row
    )
    chosen = request_ids == mine_req
    peak_score = jnp.where(chosen[:, None, None], peak_one, NEG_FILL)
    weight_sum = jnp.where(chosen[:, None, None], sum_one, 0.0)
    weighted = jnp.where(chosen[:, None, None, None], weighted_one, 0.0)
    peak_score, weight_sum, weighted = joined((peak_score, weight_sum, weighted), "seq", combine)
    select_out = finish(peak_score, weight_sum, weighted, next_query, next_key, next_value)
    return (filter_out, next_hidden, compact_cache, select_out)


def solution(mesh):
    in_specs = (
        P(None, "seq"),
        P(None, "kvh"),
        P(None, "kvh"),
        P(None, "seq", "kvh"),
        P("kvh", "seq"),
        P("seq"),
        P("seq", "kvh", None),
        P(None, "seq", "kvh"),
        P(),
        P(),
    )
    out_specs = (P(None, "kvh"), P(None, "seq"), P("seq", None, "kvh"), P(None, "kvh"))
    return jax.shard_map(
        per_device, mesh=mesh, in_specs=in_specs, out_specs=out_specs, check_vma=False
    )
```

profile of v0, /device:TPU:8, one launch (start us, length us, event | category | flops | bytes accessed | tf_op | source)
XLA Modules:
  0.0 821.8 jit_solution(1694319436126697916)
XLA Ops:
  7.2 1.7 copy.94
  10.8 1.1 fusion.11
  11.9 1.1 convert_reduce_fusion.1
  16.4 6.2 gather_fusion.1
  22.7 3.9 gather_fusion.2
  26.8 1.1 select_select_fusion
  27.9 18.6 %all-to-all-start = ((bf16[64,16,256]{2,1,0:T(8,128)(2,1)}), bf16[64,16,256]{2,1,0:T(8,128)(2,1)S(1)}, u32[]{:S(2)}, u32[]{:S(2)}) async-start(bf16[64,16,256]{2,1,0:T(8,128)(2,1)} %select_select_fusion), calls=%async_computation | async-start | bytes 1048576 | tf_op jit(solution)/shard_map/all_to_all | solution.py:168
  47.1 3.1 gather_fusion
  50.2 96.9 %all-gather.4 = f32[64,16,8]{1,2,0:T(8,128)S(1)} all-gather(f32[1,16,8]{1,2,0:T(8,128)S(1)} %bitcast.257), channel_id=3, replica_groups=mesh['seq'=64,'kvh'=8] {'seq'}, dimensions={0}, use_global_device_ids=true | all-gather | bytes 33280 | tf_op jit(solution)/shard_map/all_gather | solution.py:19
  147.2 81.2 %all-gather.3 = f32[64,16,8]{1,2,0:T(8,128)S(1)} all-gather(f32[1,16,8]{1,2,0:T(8,128)S(1)} %bitcast.256), channel_id=2, replica_groups=mesh['seq'=64,'kvh'=8] {'seq'}, dimensions={0}, use_global_device_ids=true | all-gather | bytes 33280 | tf_op jit(solution)/shard_map/all_gather | solution.py:19
  228.7 2.0 gather_fusion.3
  231.8 73.8 %while.38 = (s32[]{:T(128)}, f32[16,1,8]{0,2,1:T(8,128)S(1)}, f32[16,1,8]{0,2,1:T(8,128)S(1)}, f32[16,1,8,128]{3,2,1,0:T(8,128)S(1)}, f32[64,16,1,8]{1,3,2,0:T(8...) while((s32[]{:T(128)}, f32[16,1,8]{0,2,1:T(8,128)S(1)}, ...), condition=%wide.region_3.4_spmd, body=%wide.region_2.3_spmd.sunk | while | flops 50053 | bytes 206491 | solution.py:24
  232.0 0.9 fusion.86
  233.1 0.9 fusion.86
  234.3 0.9 fusion.86
  241.3 0.9 fusion.86
  242.5 0.9 fusion.86
  306.1 10.2 %psum.21 = f32[16,128]{1,0:T(8,128)S(1)} all-reduce(f32[16,128]{1,0:T(8,128)S(1)} %fusion.73), channel_id=1, replica_groups=mesh['seq'=64,'kvh'=8] {'kvh'}, use_global_device_ids=true, to_apply=%region_4.5 | all-reduce | flops 2048 | bytes 16384 | tf_op jit(solution)/shard_map/psum | solution.py:133
  317.4 140.6 %psum.23 = f32[16]{0:T(128)S(1)} all-reduce(f32[16]{0:T(128)S(1)} %get-tuple-element.449), channel_id=1, replica_groups=mesh['seq'=64,'kvh'=8] {'seq'}, use_global_device_ids=true, to_apply=%region_11.12 | all-reduce | flops 16 | bytes 128 | tf_op jit(solution)/shard_map/psum | solution.py:140
  458.1 116.9 %all-reduce.2.cloned.1.call-done = f32[16,1280]{1,0:T(8,128)} async-done(((f32[16,1280]{1,0:T(8,128)}), f32[16,1280]{1,0:T(8,128)}) %all-reduce.2.cloned.1.call-update) | async-done | bytes 81936 | tf_op jit(solution)/shard_map/psum | solution.py:140
  575.0 1.0 broadcast_multiply_fusion
  578.9 80.5 %all_gather.37 = f32[64,16,1,8]{1,3,2,0:T(8,128)S(1)} all-gather(f32[1,16,1,8]{1,3,2,0:T(8,128)S(1)} %get-tuple-element.469), channel_id=1, replica_groups=mesh['seq'=64,'kvh'=8] {'seq'}, dimensions={0}, use_global_device_ids=true | all-gather | bytes 33280 | tf_op jit(solution)/shard_map/all_gather | solution.py:19
  659.4 80.2 %all_gather.36 = f32[64,16,1,8]{1,3,2,0:T(8,128)S(1)} all-gather(f32[1,16,1,8]{1,3,2,0:T(8,128)S(1)} %get-tuple-element.470), channel_id=1, replica_groups=mesh['seq'=64,'kvh'=8] {'seq'}, dimensions={0}, use_global_device_ids=true | all-gather | bytes 33280 | tf_op jit(solution)/shard_map/all_gather | solution.py:19
  740.5 73.8 %while.39 = (s32[]{:T(128)}, f32[16,1,8]{0,2,1:T(8,128)S(1)}, f32[16,1,8]{0,2,1:T(8,128)S(1)}, f32[16,1,8,128]{3,2,1,0:T(8,128)S(1)}, f32[64,16,1,8]{1,3,2,0:T(8...) while((s32[]{:T(128)}, f32[16,1,8]{0,2,1:T(8,128)S(1)}, ...), condition=%wide.region_15.16_spmd, body=%wide.region_14.15_spmd.sunk | while | flops 50053 | bytes 206491 | solution.py:24
  (869 shorter events, 150.6 us)
Async XLA Ops:
  7.2 15.5 %copy-start = (bf16[16,128,256]{2,1,0:T(8,128)(2,1)S(1)}, bf16[16,128,256]{2,1,0:T(8,128)(2,1)}, u32[]{:S(2)}) copy-start(bf16[16,128,256]{2,1,0:T(8,128)(2,1)} %param.21) | copy-start | bytes 3145732
  7.2 223.8 %all-gather.10.cloned.1.call-start = ((), (), s32[]{:S(2)}) async-start(), calls=%async_computation.3 | async-start | bytes 4259840 | tf_op jit(solution)/shard_map/all_gather | solution.py:19
  22.5 24.0 %copy-start.5 = (bf16[16,256]{1,0:T(8,128)(2,1)S(1)}, bf16[16,256]{1,0:T(8,128)(2,1)}, u32[]{:S(2)}) copy-start(bf16[16,256]{1,0:T(8,128)(2,1)} %param.16) | copy-start | bytes 24580
  22.5 24.4 %copy-start.8 = (s32[16]{0:T(128)S(1)}, s32[16]{0:T(128)}, u32[]{:S(2)}) copy-start(s32[16]{0:T(128)} %param.22) | copy-start | bytes 196
  27.9 200.8 %all-to-all-start = ((bf16[64,16,256]{2,1,0:T(8,128)(2,1)}), bf16[64,16,256]{2,1,0:T(8,128)(2,1)S(1)}, u32[]{:S(2)}, u32[]{:S(2)}) async-start(bf16[64,16,256]{2,1,0:T(8,128)(2,1)} %select_select_fusion), calls=%async_computation | async-start | bytes 1048576 | tf_op jit(solution)/shard_map/all_to_all | solution.py:168
  46.5 528.5 %all-reduce.2.cloned.1.call-start = ((), (), s32[]{:S(2)}) async-start(), calls=%async_computation.1 | async-start | bytes 163840 | tf_op jit(solution)/shard_map/psum | solution.py:140
  46.7 259.2 %copy-start.2 = (bf16[1024,128]{1,0:T(8,128)(2,1)S(1)}, bf16[1024,128]{1,0:T(8,128)(2,1)}, u32[]{:S(2)}) copy-start(bf16[1024,128]{1,0:T(8,128)(2,1)} %param.18) | copy-start | bytes 786436
  47.1 269.3 %copy-start.6 = (bf16[16,128]{1,0:T(8,128)(2,1)S(1)}, bf16[16,128]{1,0:T(8,128)(2,1)}, u32[]{:S(2)}) copy-start(bf16[16,128]{1,0:T(8,128)(2,1)} %param.14) | copy-start | bytes 12292
  47.1 269.4 %copy-start.1 = (bf16[128,1,1280]{2,0,1:T(8,128)(2,1)S(1)}, bf16[128,1,1280]{2,0,1:T(8,128)(2,1)}, u32[]{:S(2)}) copy-start(bf16[128,1,1280]{2,0,1:T(8,128)(2,1)} %param.20) | copy-start | bytes 983044
  47.1 269.4 %copy-start.7 = (f32[128]{0:T(128)S(1)}, f32[128]{0:T(128)}, u32[]{:S(2)}) copy-start(f32[128]{0:T(128)} %param.19) | copy-start | bytes 1540
  305.9 509.3 %copy-start.3 = (bf16[2,8,8,128]{3,1,2,0:T(8,128)(2,1)}, bf16[2,8,8,128]{3,1,2,0:T(8,128)(2,1)S(1)}, u32[]{:S(2)}) copy-start(bf16[2,8,8,128]{3,1,2,0:T(8,128)(2,1)S(1)} %copy.128) | copy-start | bytes 98308
  316.5 498.8 %copy-start.4 = (bf16[16,128]{1,0:T(8,128)(2,1)}, bf16[16,128]{1,0:T(8,128)(2,1)S(1)}, u32[]{:S(2)}) copy-start(bf16[16,128]{1,0:T(8,128)(2,1)S(1)} %get-tuple-element.450) | copy-start | bytes 12292
  317.4 422.3 %all-gather.8.cloned.1.call-start = ((), (), s32[]{:S(2)}) async-start(), calls=%async_computation.2 | async-start | bytes 4259840 | tf_op jit(solution)/shard_map/all_gather | solution.py:19
Sparse Core Ops, SparseCore 0:
  12.0 156.1 all-gather.9
  317.5 257.4 all-reduce.1
  577.9 141.6 all-gather.7
where the time goes:
time: 828 us; the launch traced here: 822 us
  blocking collectives  490 us (59%)
  other arithmetic  131 us (16%)
  waiting for transfers between devices  117 us (14%)
  local copies, waits for them, and re-layouts  42.3 us (5%)
  starting transfers between devices  18.7 us (2%)
  between operations  14.3 us (2%)
    all_gather x4, blocking collectives, joined(): gathered = jax.tree.map(lambda a: lax.all_gather(a, axis), part)  339 us
    psum x1, blocking collectives, per_device(): lax.psum((projected, jnp.sum(widened * widened, axis=1)), 'seq')  141 us
    add x126, other arithmetic, combine(): weighted = left[2] * left_fade[..., None] + right[2] * right_fade[..., None]  119 us
    psum x1, waiting for transfers between devices, per_device(): lax.psum((projected, jnp.sum(widened * widened, axis=1)), 'seq')  117 us
    all_to_all x1, starting transfers between devices, per_device(): lax.all_to_all(outgoing, 'seq', split_axis=0, concat_axis=0, tiled=True)  18.6 us
    mul x252, local copies, waits for them, and re-layouts, combine(): weighted = left[2] * left_fade[..., None] + right[2] * right_fade[..., None]  18 us
  transfers between devices with their start and end apart: 4, of which 1 were waited for; matrix products, arithmetic and copies ran while one was open for 3% of the time, Pallas kernels for 0%

commit v1 on v0

v1 whole, which is shorter than its diff:
```python
import functools
import math

import jax
import jax.numpy as jnp
import numpy as np
from jax import lax
from jax.experimental import pallas as pl
from jax.experimental.pallas import tpu as pltpu
from jax.sharding import PartitionSpec as P

D = 8192
HD = 128
SEL = 2048
REQS = 16
HEADS = 8
ROWS = 128
NEG_FILL = -1e30
ROPE_BASE = 500000.0
EPSILON = 1e-05
SCALE = 1.0 / math.sqrt(HD)
MESH = pl.DeviceIdType.MESH
FAR_FIRST = (8, 7, 9, 6, 10, 5, 11, 4, 12, 3, 13, 2, 14, 1, 15)
F32 = jnp.float32
BF16 = jnp.bfloat16
WINDOWS = (0, 16, 28, 44, 60)


def nt_dot(a, b):
    return lax.dot_general(a, b, (((1,), (1,)), ((), ())), preferred_element_type=F32)


def iota(shape, axis):
    return lax.broadcasted_iota(jnp.int32, shape, axis)


def wait_bytes(view, sem):
    pltpu.make_async_copy(view, view, sem).wait()


def step(
    hidden_h, fq_h, ne_h, fc_h, ow_h, gain_h, nw_h, nc_h, lens, sel_h, inv_h,
    fo_o, nh_o, cc_o, so_o,
    hidden, fq, ne, fc, ow, gain, nw, nc, sel, inv,
    qs, bs, br, onehot, comp,
    axs, axms, axr, axmr, azs, azms, azr, azmr, foxs, fox,
    ybs, ybr, cxs, cxr, czs, czr, cas, car, dxs, dxr, fins, fin,
    in_sem, s_sem, r_sem, m_sem, out_sem,
):
    seq = lax.axis_index("seq")
    kv = lax.axis_index("kvh")
    z, x = seq // 4, seq % 4
    base = seq * ROWS

    loads = {}
    for i, (name, src, dst) in enumerate((
        ("fq", fq_h, fq), ("fc", fc_h, fc), ("sel", sel_h, sel), ("nc", nc_h, nc), ("ne", ne_h, ne),
        ("ow", ow_h, ow), ("hidden", hidden_h, hidden), ("gain", gain_h, gain), ("nw", nw_h, nw), ("inv", inv_h, inv),
    )):
        loads[name] = pltpu.make_async_copy(src, dst, in_sem.at[i])
        loads[name].start()

    barrier = pltpu.get_barrier_semaphore()

    def greet(d, carry):
        pl.semaphore_signal(barrier, inc=1, device_id=((seq + d) % 64, kv), device_id_type=MESH)
        return carry

    lax.fori_loop(1, 64, greet, 0)
    for d in range(1, 8):
        pl.semaphore_signal(barrier, inc=1, device_id=(seq, (kv + d) % 8), device_id_type=MESH)

    def push(src, dst, sem, target):
        pltpu.make_async_remote_copy(
            src_ref=src, dst_ref=dst, send_sem=s_sem.at[sem], recv_sem=r_sem.at[sem],
            device_id=target, device_id_type=MESH,
        ).start()

    def x_peer(d):
        return (x + d) % 4

    def at_x(p):
        return (z * 4 + p, kv)

    def at_z(p):
        return (p * 4 + x, kv)

    loads["fq"].wait()
    loads["fc"].wait()
    for c in range(4):
        qs[c] = jnp.concatenate(
            [fq[:, (2 * c + i) * HD : (2 * c + i + 1) * HD] for i in range(2)], axis=0
        )
    query = qs[...].reshape(HEADS * REQS, HD)
    keys = fc[:, :, 0:HD].reshape(REQS * ROWS, HD)
    values = fc[:, :, HD : 2 * HD].reshape(REQS * ROWS, HD)
    lane1 = iota((1, ROWS), 1)
    row_req = iota((HEADS * REQS, ROWS), 0) % REQS
    scores = nt_dot(query, keys) * SCALE
    masked, alive = [], []
    for r in range(REQS):
        live = jnp.where((lane1 + base) < lens[r], r, -1)
        ok = row_req == live
        alive.append(ok)
        masked.append(jnp.where(ok, scores[:, r * ROWS : (r + 1) * ROWS], NEG_FILL))
    peak = masked[0]
    for r in range(1, REQS):
        peak = jnp.maximum(peak, masked[r])
    peak = jnp.max(peak, axis=1, keepdims=True)
    total = jnp.zeros((HEADS * REQS, ROWS), F32)
    weights = []
    for r in range(REQS):
        w = jnp.where(alive[r], jnp.exp(masked[r] - peak), 0.0)
        total = total + w
        weights.append(w.astype(BF16))
    total = jnp.sum(total, axis=1, keepdims=True)
    number = jnp.dot(jnp.concatenate(weights, axis=1), values, preferred_element_type=F32)
    axs[...] = number.astype(BF16).reshape(4, 32, HD)
    lane = iota((HEADS * REQS, HD), 1)
    sub = iota((HEADS * REQS, HD), 0) % 32
    spread = jnp.where(lane == sub, peak, 0.0) + jnp.where(lane == sub + 32, total, 0.0)
    axms[...] = jnp.sum(spread.reshape(4, 32, HD), axis=1, keepdims=True)

    loads["sel"].wait()
    loads["nc"].wait()
    below = jnp.zeros((REQS, 128), F32)
    upto = jnp.zeros((REQS, 128), F32)
    for c in range(SEL // 128):
        chunk = sel[:, c * 128 : (c + 1) * 128]
        below = below + jnp.where(chunk < base, 1.0, 0.0)
        upto = upto + jnp.where(chunk < base + ROWS, 1.0, 0.0)
    first = jnp.sum(below, axis=1, keepdims=True).astype(jnp.int32)
    last = jnp.sum(upto, axis=1, keepdims=True).astype(jnp.int32)
    chunk0 = first >> 7
    win = [jnp.zeros((REQS, 128), jnp.int32) for _ in range(2)]
    for c in range(SEL // 128):
        chunk = sel[:, c * 128 : (c + 1) * 128]
        win[0] = win[0] + jnp.where(chunk0 == c, chunk, 0)
        win[1] = win[1] + jnp.where(chunk0 == c - 1, chunk, 0)
    entry = jnp.concatenate(
        [chunk0 * 128 + iota((REQS, 128), 1), chunk0 * 128 + 128 + iota((REQS, 128), 1)], axis=1
    )
    usable = (entry >= first) & (entry < last)
    slot = jnp.where(usable, (entry & 3) * 16 + ((entry - first) >> 2), -1)
    place = jnp.where(usable, jnp.concatenate(win, axis=1) - base, -1)
    slot_id = iota((64, 256), 0)
    row_id = iota((ROWS, 256), 0)
    for r in range(REQS):
        hit = jnp.where(slot_id == slot[r : r + 1, :], 1.0, 0.0).astype(BF16)
        row = jnp.where(row_id == place[r : r + 1, :], 1.0, 0.0).astype(BF16)
        choose = nt_dot(hit, row).astype(BF16)
        packed = jnp.dot(choose, nc[r], preferred_element_type=F32)
        bs[4 * r : 4 * r + 4] = packed.astype(BF16).reshape(4, 16, 2 * HD)

    pl.semaphore_wait(barrier, 70)

    def rows_window(w):
        def send(i, carry):
            n = i // 4
            dz = jnp.where(n % 2 == 1, 8 - (n + 1) // 2, 8 + n // 2)
            t = ((z + dz) % 16) * 4 + (x + i) % 4
            push(bs.at[t], br.at[seq], 0, (t, kv))
            return carry

        lax.fori_loop(WINDOWS[w], WINDOWS[w + 1], send, 0)
        if w == len(WINDOWS) - 2:
            lax.fori_loop(61, 64, send, 0)

    for d in (2, 1, 3):
        p = x_peer(d)
        push(axs.at[p], axr.at[x], 1, at_x(p))
        push(axms.at[p], axmr.at[x], 2, at_x(p))
    axr[x] = axs[x]
    axmr[x] = axms[x]
    rows_window(0)
    mine = sel[pl.ds(z, 1), :]
    src_col = iota((64, SEL), 0)
    starts = jnp.sum(jnp.where(mine < src_col * ROWS, 1.0, 0.0), axis=1, keepdims=True)
    ends = jnp.sum(jnp.where(mine < (src_col + 1) * ROWS, 1.0, 0.0), axis=1, keepdims=True)
    own_lane = iota((64, 1024), 1) >> 4 == iota((64, 1024), 0)
    starts = jnp.sum(jnp.where(own_lane, starts, 0.0), axis=0, keepdims=True).astype(jnp.int32)
    ends = jnp.sum(jnp.where(own_lane, ends, 0.0), axis=0, keepdims=True).astype(jnp.int32)
    index = starts + ((x - starts) & 3) + 4 * (iota((1, 1024), 1) & 15)
    target_row = jnp.where(index < ends, index >> 2, -1)
    for c in range(4):
        onehot[c * 128 : (c + 1) * 128, :] = jnp.where(
            iota((128, 1024), 0) + c * 128 == target_row, 1.0, 0.0
        ).astype(BF16)

    def recv(view, sem):
        wait_bytes(view, r_sem.at[sem])

    def merge(count, part, stats):
        table = stats[...].reshape(count, HD).T
        peaks, sums = table[0:32], table[32:64]
        top = jnp.max(peaks, axis=1, keepdims=True)
        fade = jnp.exp(peaks - top)
        mass = jnp.sum(fade * sums, axis=1, keepdims=True)
        acc = fade[:, 0:1] * part[0].astype(F32)
        for s in range(1, count):
            acc = acc + fade[:, s : s + 1] * part[s].astype(F32)
        return top, mass, acc

    recv(axr.at[pl.ds(0, 3)], 1)
    recv(axmr.at[pl.ds(0, 3)], 2)
    top, mass, acc = merge(4, axr, axmr)
    azs[...] = acc.astype(BF16)
    lane = iota((32, HD), 1)
    sub = iota((32, HD), 0)
    spread = jnp.where(lane == sub, top, 0.0) + jnp.where(lane == sub + 32, mass, 0.0)
    azms[...] = jnp.sum(spread, axis=0, keepdims=True)

    for d in FAR_FIRST:
        p = (z + d) % 16
        push(azs, azr.at[z], 3, at_z(p))
        push(azms, azmr.at[z], 4, at_z(p))
    azr[z] = azs[...]
    azmr[z] = azms[...]
    rows_window(1)
    loads["ne"].wait()
    fresh_key = jnp.concatenate([ne[:, 0:HD]] * 2, axis=0).astype(F32)
    fresh_value = jnp.concatenate([ne[:, HD : 2 * HD]] * 2, axis=0).astype(F32)
    own = jnp.sum(qs[x].astype(F32) * fresh_key, axis=1, keepdims=True) * SCALE
    recv(azr.at[pl.ds(0, 15)], 3)
    recv(azmr.at[pl.ds(0, 15)], 4)

    def close(top, mass, acc, own, fresh_value):
        peak = jnp.maximum(top, own)
        fade = jnp.exp(top - peak)
        mine = jnp.exp(own - peak)
        acc = acc * fade + mine.astype(BF16).astype(F32) * fresh_value
        return (acc / (mass * fade + mine)).astype(BF16)

    top, mass, acc = merge(16, azr, azmr)
    foxs[...] = close(top, mass, acc, own, fresh_value)
    for d in (2, 1, 3):
        p = x_peer(d)
        push(foxs, fox.at[x], 5, at_x(p))
    fox[x] = foxs[...]
    rows_window(2)
    loads["ow"].wait()
    loads["hidden"].wait()
    loads["gain"].wait()
    loads["nw"].wait()
    loads["inv"].wait()
    recv(fox.at[pl.ds(0, 3)], 5)
    out_rows = jnp.concatenate(
        [fox[h // 2, (h % 2) * 16 : (h % 2) * 16 + 16] for h in range(HEADS)], axis=1
    )
    ybs[...] = jnp.dot(out_rows, ow[...], preferred_element_type=F32)
    for d in (4, 3, 5, 2, 6, 1, 7):
        push(ybs, ybr.at[kv], 6, (seq, (kv + d) % 8))
    ybr[kv] = ybs[...]
    fo_o[...] = out_rows
    recv(ybr.at[pl.ds(0, 7)], 6)
    mixed = ybr[0]
    for i in range(1, 8):
        mixed = mixed + ybr[i]
    next_hidden = (hidden[...].astype(F32) + mixed).astype(BF16)
    nh_o[...] = next_hidden
    wide = next_hidden.astype(F32)
    scaled = (wide * gain[...]).astype(BF16)
    squares = jnp.sum(wide * wide, axis=1, keepdims=True)
    projected = jnp.dot(scaled, nw[...], preferred_element_type=F32)
    for b in range(10):
        cxs[b // 3, b % 3] = projected[:, b * HD : (b + 1) * HD]
    cxs[3, 1] = jnp.broadcast_to(squares, (REQS, HD))
    cxs[3, 2] = jnp.zeros((REQS, HD), F32)
    for d in (2, 1, 3):
        p = x_peer(d)
        push(cxs.at[p], cxr.at[x], 7, at_x(p))
    cxr[x] = cxs[x]
    rows_window(3)
    recv(cxr.at[pl.ds(0, 3)], 7)
    summed = cxr[0] + cxr[1] + cxr[2] + cxr[3]
    czs[...] = summed.reshape(3, REQS, 1, HD)
    for d in FAR_FIRST:
        p = (z + d) % 16
        push(czs.at[:, p], czr.at[z], 8, at_z(p))
    czr[z] = czs[:, z]
    angle = lens[z].astype(F32) * inv[...]
    cosine = jnp.cos(angle)
    sine = jnp.where(iota((1, HD), 1) < HD // 2, -jnp.sin(angle), jnp.sin(angle))
    recv(czr.at[pl.ds(0, 15)], 8)
    summed = czr[0]
    for s in range(1, 16):
        summed = summed + czr[s]
    cas[...] = summed
    for d in (2, 1, 3):
        p = x_peer(d)
        push(cas, car.at[x], 9, at_x(p))
    car[x] = cas[...]
    recv(car.at[pl.ds(0, 3)], 9)
    br[seq] = bs[seq]
    recv(br.at[pl.ds(0, 63)], 0)
    arrived = br[...].reshape(1024, 2 * HD)
    comp[...] = jnp.dot(onehot[...], arrived, preferred_element_type=F32).astype(BF16)
    compact_out = pltpu.make_async_copy(comp, cc_o.at[0], out_sem.at[0])
    compact_out.start()
    mine = car[...].reshape(12, HD)
    norm = lax.rsqrt(mine[10:11] / D + EPSILON)
    mine = mine * norm
    turned = mine * cosine + pltpu.roll(mine, HD // 2, 1) * sine
    next_query = turned[0:8].astype(BF16)
    next_key = turned[8:9].astype(BF16).astype(F32)
    next_value = mine[9:10].astype(BF16).astype(F32)
    scores = nt_dot(next_query, comp[:, 0:HD]) * SCALE
    peak = jnp.max(scores, axis=1, keepdims=True)
    weights = jnp.exp(scores - peak)
    total = jnp.sum(weights, axis=1, keepdims=True)
    number = jnp.dot(weights.astype(BF16), comp[:, HD : 2 * HD], preferred_element_type=F32)
    dxs[0:8] = number
    dxs[8:16] = jnp.where(iota((8, HD), 1) < 64, peak, total)
    for d in (2, 1, 3):
        p = x_peer(d)
        push(dxs, dxr.at[x], 10, at_x(p))
    dxr[x] = dxs[...]
    own = jnp.sum(next_query.astype(F32) * next_key, axis=1, keepdims=True) * SCALE
    recv(dxr.at[pl.ds(0, 3)], 10)
    peaks = [dxr[s, 8:16, 0:1] for s in range(4)]
    top = jnp.maximum(jnp.maximum(peaks[0], peaks[1]), jnp.maximum(peaks[2], peaks[3]))
    mass = jnp.zeros((8, 1), F32)
    acc = jnp.zeros((8, HD), F32)
    for s in range(4):
        fade = jnp.exp(peaks[s] - top)
        mass = mass + fade * dxr[s, 8:16, 64:65]
        acc = acc + fade * dxr[s, 0:8]
    fins[...] = close(top, mass, acc, own, next_value).astype(F32)
    for d in FAR_FIRST:
        p = (z + d) % 16
        push(fins, fin.at[z], 11, at_z(p))
    fin[z] = fins[...]

    def sent(view, sem):
        wait_bytes(view, s_sem.at[sem])

    sent(br.at[pl.ds(0, 63)], 0)
    sent(axr.at[pl.ds(0, 3)], 1)
    sent(axmr.at[pl.ds(0, 3)], 2)
    sent(azr.at[pl.ds(0, 15)], 3)
    sent(azmr.at[pl.ds(0, 15)], 4)
    sent(fox.at[pl.ds(0, 3)], 5)
    sent(ybr.at[pl.ds(0, 7)], 6)
    sent(cxr.at[pl.ds(0, 3)], 7)
    sent(czr.at[pl.ds(0, 15)], 8)
    sent(car.at[pl.ds(0, 3)], 9)
    sent(dxr.at[pl.ds(0, 3)], 10)
    compact_out.wait()
    recv(fin.at[pl.ds(0, 15)], 11)
    for h in range(HEADS):
        so_o[:, h * HD : (h + 1) * HD] = fin[:, h, :].astype(BF16)
    sent(fin.at[pl.ds(0, 15)], 11)


def per_device(
    hidden, filter_query, new_entry, filter_cache, out_weight, next_gain, next_weight, next_cache,
    lengths, selected,
):
    rate = (1.0 / ROPE_BASE ** (np.arange(HD // 2) * 2.0 / HD)).astype(np.float32)
    inverse = jnp.asarray(np.concatenate([rate, rate])[None, :])
    hbm = pl.BlockSpec(memory_space=pl.ANY)
    vmem = pl.BlockSpec(memory_space=pltpu.VMEM)
    smem = pl.BlockSpec(memory_space=pltpu.SMEM)
    v = pltpu.VMEM
    return pl.pallas_call(
        step,
        out_shape=(
            jax.ShapeDtypeStruct((REQS, HEADS * HD), BF16),
            jax.ShapeDtypeStruct((REQS, HD), BF16),
            jax.ShapeDtypeStruct((1, 512, 2 * HD), BF16),
            jax.ShapeDtypeStruct((REQS, HEADS * HD), BF16),
        ),
        in_specs=[hbm] * 8 + [smem, hbm, hbm],
        out_specs=(vmem, vmem, hbm, vmem),
        scratch_shapes=[
            v((REQS, HD), BF16), v((REQS, HEADS * HD), BF16), v((REQS, 2 * HD), BF16),
            v((REQS, ROWS, 2 * HD), BF16), v((HEADS * HD, HD), BF16), v((1, HD), F32), v((HD, 10 * HD), BF16),
            v((REQS, ROWS, 2 * HD), BF16), v((REQS, SEL), jnp.int32), v((1, HD), F32),
            v((4, 32, HD), BF16), v((64, 16, 2 * HD), BF16), v((64, 16, 2 * HD), BF16),
            v((512, 1024), BF16), v((512, 2 * HD), BF16),
            v((4, 32, HD), BF16), v((4, 1, HD), F32), v((4, 32, HD), BF16), v((4, 1, HD), F32),
            v((32, HD), BF16), v((1, HD), F32), v((16, 32, HD), BF16), v((16, 1, HD), F32),
            v((32, HD), BF16), v((4, 32, HD), BF16),
            v((REQS, HD), F32), v((8, REQS, HD), F32),
            v((4, 3, REQS, HD), F32), v((4, 3, REQS, HD), F32),
            v((3, REQS, 1, HD), F32), v((16, 3, 1, HD), F32),
            v((3, 1, HD), F32), v((4, 3, 1, HD), F32),
            v((16, HD), F32), v((4, 16, HD), F32),
            v((8, HD), F32), v((16, 8, HD), F32),
            pltpu.SemaphoreType.DMA((10,)), pltpu.SemaphoreType.DMA((12,)), pltpu.SemaphoreType.DMA((12,)),
            pltpu.SemaphoreType.DMA((1,)), pltpu.SemaphoreType.DMA((1,)),
        ],
        compiler_params=pltpu.CompilerParams(
            collective_id=0, has_side_effects=True, vmem_limit_bytes=60 * 1024 * 1024
        ),
        name="decode_step",
    )(
        hidden, filter_query, new_entry, filter_cache, out_weight, next_gain.reshape(1, -1),
        next_weight.reshape(next_weight.shape[0], -1), next_cache, lengths, selected, inverse,
    )


def solution(mesh):
    in_specs = (
        P(None, "seq"),
        P(None, "kvh"),
        P(None, "kvh"),
        P(None, "seq", "kvh"),
        P("kvh", "seq"),
        P("seq"),
        P("seq", "kvh", None),
        P(None, "seq", "kvh"),
        P(),
        P(),
    )
    out_specs = (P(None, "kvh"), P(None, "seq"), P("seq", None, "kvh"), P(None, "kvh"))
    return jax.shard_map(
        per_device, mesh=mesh, in_specs=in_specs, out_specs=out_specs, check_vma=False
    )
```

time: 828 us -> 80.5 us (0.10)
  the two profiles are of different devices: /device:TPU:8 before, /device:TPU:2 now
where the time goes in v1:
time: 80.5 us; the launch traced here: 80.3 us
  Pallas kernels  75.3 us (94%)
  local copies, waits for them, and re-layouts  4.27 us (5%)
    pallas_call x1, Pallas kernels, per_device(): pl.pallas_call(step, out_shape=(jax.ShapeDtypeStruct((REQS, HEADS * HD),...  75.3 us
    unnamed x8, local copies, waits for them, and re-layouts  4.27 us

profile of v1, /device:TPU:2, one launch (start us, length us, event | category | flops | bytes accessed | tf_op | source)
XLA Modules:
  0.0 80.3 jit_solution(189804004160703020)
XLA Ops:
  0.6 75.3 %decode_step.1 = (bf16[16,1024]{1,0:T(8,128)(2,1)}, bf16[16,128]{1,0:T(8,128)(2,1)}, bf16[1,512,256]{2,1,0:T(8,128)(2,1)}, bf16[16,1024]{1,0:T(8,128)(2,1)}) custom-call(bf16[16,128]{1,0:T(8,128)(2,1)} %hidden_h.1, bf16[16,1024]{1,0:T(8,128)(2,1)} %fq_h.1, bf16[16,256]{1,0:T(8,128)(2,1)} %ne_h.1, bf16[16,128,256]{2,1,0:T(8,128)(2,1)} %fc_h.1, ...), custom_call_target="tpu_custom_call" | custom-call | tf_op jit(solution)/shard_map/decode_step/pallas_call | solution.py:365
  76.0 0.0 copy-start.1
  76.0 1.4 %copy.19 = bf16[16,1024]{1,0:T(8,128)(2,1)} copy(bf16[16,1024]{1,0:T(8,128)(2,1)} %get-tuple-element.8) | data formatting | bytes 65536
  77.4 0.0 copy-done.1
  77.4 0.6 copy.20
  78.0 0.0 copy-start
  78.0 1.7 %copy.21 = bf16[1,512,256]{2,1,0:T(8,128)(2,1)} copy(bf16[1,512,256]{2,1,0:T(8,128)(2,1)} %get-tuple-element.10) | data formatting | bytes 524288
  79.6 0.0 copy-done
  79.6 0.6 copy.22
Async XLA Ops:
  76.0 1.4 %copy-start.1 = (bf16[16,128]{1,0:T(8,128)(2,1)S(1)}, bf16[16,128]{1,0:T(8,128)(2,1)}, u32[]{:S(2)}) copy-start(bf16[16,128]{1,0:T(8,128)(2,1)} %get-tuple-element.9) | copy-start | bytes 12292
  78.0 1.7 %copy-start = (bf16[16,1024]{1,0:T(8,128)(2,1)S(1)}, bf16[16,1024]{1,0:T(8,128)(2,1)}, u32[]{:S(2)}) copy-start(bf16[16,1024]{1,0:T(8,128)(2,1)} %get-tuple-element.11) | copy-start | bytes 98308

commit v2 on v1

--- a/solution.py
+++ b/solution.py
@@ -23,7 +23,8 @@
 FAR_FIRST = (8, 7, 9, 6, 10, 5, 11, 4, 12, 3, 13, 2, 14, 1, 15)
 F32 = jnp.float32
 BF16 = jnp.bfloat16
-WINDOWS = (0, 16, 28, 44, 60)
+YT = BF16
+WINDOWS = (0, 4, 32, 60, 60)
 
 
 def nt_dot(a, b):
@@ -41,10 +42,10 @@
 def step(
     hidden_h, fq_h, ne_h, fc_h, ow_h, gain_h, nw_h, nc_h, lens, sel_h, inv_h,
     fo_o, nh_o, cc_o, so_o,
-    hidden, fq, ne, fc, ow, gain, nw, nc, sel, inv,
+    hidden, fq, ne, fc, owx, gain, nw, nc, sel, inv,
     qs, bs, br, onehot, comp,
     axs, axms, axr, axmr, azs, azms, azr, azmr, foxs, fox,
-    ybs, ybr, cxs, cxr, czs, czr, cas, car, dxs, dxr, fins, fin,
+    ybs, ybr, cxs, cxr, czs, czr, car, dxs, dxr, fins, fin,
     in_sem, s_sem, r_sem, m_sem, out_sem,
 ):
     seq = lax.axis_index("seq")
@@ -55,7 +56,7 @@
     loads = {}
     for i, (name, src, dst) in enumerate((
         ("fq", fq_h, fq), ("fc", fc_h, fc), ("sel", sel_h, sel), ("nc", nc_h, nc), ("ne", ne_h, ne),
-        ("ow", ow_h, ow), ("hidden", hidden_h, hidden), ("gain", gain_h, gain), ("nw", nw_h, nw), ("inv", inv_h, inv),
+        ("ow", ow_h.at[pl.ds(pl.multiple_of(x * 256, 256), 256)], owx.at[x]), ("hidden", hidden_h, hidden), ("gain", gain_h, gain), ("nw", nw_h, nw), ("inv", inv_h, inv),
     )):
         loads[name] = pltpu.make_async_copy(src, dst, in_sem.at[i])
         loads[name].start()
@@ -67,8 +68,14 @@
         return carry
 
     lax.fori_loop(1, 64, greet, 0)
-    for d in range(1, 8):
-        pl.semaphore_signal(barrier, inc=1, device_id=(seq, (kv + d) % 8), device_id_type=MESH)
+
+    def greet_heads(i, carry):
+        pl.semaphore_signal(
+            barrier, inc=1, device_id=(z * 4 + i % 4, (kv + 1 + i // 4) % 8), device_id_type=MESH
+        )
+        return carry
+
+    lax.fori_loop(0, 28, greet_heads, 0)
 
     def push(src, dst, sem, target):
         pltpu.make_async_remote_copy(
@@ -152,7 +159,7 @@
         packed = jnp.dot(choose, nc[r], preferred_element_type=F32)
         bs[4 * r : 4 * r + 4] = packed.astype(BF16).reshape(4, 16, 2 * HD)
 
-    pl.semaphore_wait(barrier, 70)
+    pl.semaphore_wait(barrier, 91)
 
     def rows_window(w):
         def send(i, carry):
@@ -172,6 +179,9 @@
         push(axms.at[p], axmr.at[x], 2, at_x(p))
     axr[x] = axs[x]
     axmr[x] = axms[x]
+    for d in (2, 1, 3):
+        p = x_peer(d)
+        push(ow_h.at[pl.ds(pl.multiple_of(p * 256, 256), 256)], owx.at[x], 9, at_x(p))
     rows_window(0)
     mine = sel[pl.ds(z, 1), :]
     src_col = iota((64, SEL), 0)
@@ -232,30 +242,36 @@
         return (acc / (mass * fade + mine)).astype(BF16)
 
     top, mass, acc = merge(16, azr, azmr)
-    foxs[...] = close(top, mass, acc, own, fresh_value)
+    heads = close(top, mass, acc, own, fresh_value)
+    foxs[...] = heads
+    loads["ow"].wait()
+    recv(owx.at[pl.ds(0, 3)], 9)
+    pair = jnp.concatenate([heads[0:16], heads[16:32]], axis=1)
+    for p in range(4):
+        ybs[p] = jnp.dot(pair, owx[p], preferred_element_type=F32).astype(YT)
+
+    def to_columns(i, carry):
+        p = (x + 3 - i % 4) % 4
+        push(ybs.at[p], ybr.at[x * 8 + kv], 6, (z * 4 + p, (kv + 4 + i // 4) % 8))
+        return carry
+
+    lax.fori_loop(0, 16, to_columns, 0)
+    lax.fori_loop(20, 32, to_columns, 0)
+    lax.fori_loop(16, 19, to_columns, 0)
+    ybr[x * 8 + kv] = ybs[x]
     for d in (2, 1, 3):
         p = x_peer(d)
         push(foxs, fox.at[x], 5, at_x(p))
     fox[x] = foxs[...]
     rows_window(2)
-    loads["ow"].wait()
     loads["hidden"].wait()
     loads["gain"].wait()
     loads["nw"].wait()
     loads["inv"].wait()
-    recv(fox.at[pl.ds(0, 3)], 5)
-    out_rows = jnp.concatenate(
-        [fox[h // 2, (h % 2) * 16 : (h % 2) * 16 + 16] for h in range(HEADS)], axis=1
-    )
-    ybs[...] = jnp.dot(out_rows, ow[...], preferred_element_type=F32)
-    for d in (4, 3, 5, 2, 6, 1, 7):
-        push(ybs, ybr.at[kv], 6, (seq, (kv + d) % 8))
-    ybr[kv] = ybs[...]
-    fo_o[...] = out_rows
-    recv(ybr.at[pl.ds(0, 7)], 6)
-    mixed = ybr[0]
-    for i in range(1, 8):
-        mixed = mixed + ybr[i]
+    recv(ybr.at[pl.ds(0, 31)], 6)
+    mixed = ybr[0].astype(F32)
+    for i in range(1, 32):
+        mixed = mixed + ybr[i].astype(F32)
     next_hidden = (hidden[...].astype(F32) + mixed).astype(BF16)
     nh_o[...] = next_hidden
     wide = next_hidden.astype(F32)
@@ -271,26 +287,32 @@
         push(cxs.at[p], cxr.at[x], 7, at_x(p))
     cxr[x] = cxs[x]
     rows_window(3)
+    recv(fox.at[pl.ds(0, 3)], 5)
+    for h in range(HEADS):
+        fo_o[:, h * HD : (h + 1) * HD] = fox[h // 2, (h % 2) * 16 : (h % 2) * 16 + 16]
     recv(cxr.at[pl.ds(0, 3)], 7)
     summed = cxr[0] + cxr[1] + cxr[2] + cxr[3]
     czs[...] = summed.reshape(3, REQS, 1, HD)
-    for d in FAR_FIRST:
-        p = (z + d) % 16
-        push(czs.at[:, p], czr.at[z], 8, at_z(p))
-    czr[z] = czs[:, z]
+
+    def to_owner(i, carry):
+        n = i // 4
+        dz = jnp.where(n % 2 == 1, 8 - (n + 1) // 2, 8 + n // 2)
+        zt = (z + dz) % 16
+        push(czs.at[:, zt], czr.at[seq], 8, (zt * 4 + (x + i) % 4, kv))
+        return carry
+
+    lax.fori_loop(0, 60, to_owner, 0)
+    lax.fori_loop(61, 64, to_owner, 0)
+    czr[seq] = czs[:, z]
     angle = lens[z].astype(F32) * inv[...]
     cosine = jnp.cos(angle)
     sine = jnp.where(iota((1, HD), 1) < HD // 2, -jnp.sin(angle), jnp.sin(angle))
-    recv(czr.at[pl.ds(0, 15)], 8)
-    summed = czr[0]
-    for s in range(1, 16):
-        summed = summed + czr[s]
-    cas[...] = summed
-    for d in (2, 1, 3):
-        p = x_peer(d)
-        push(cas, car.at[x], 9, at_x(p))
-    car[x] = cas[...]
-    recv(car.at[pl.ds(0, 3)], 9)
+    recv(czr.at[pl.ds(0, 63)], 8)
+    for p in range(4):
+        summed = czr[p]
+        for s in range(1, 16):
+            summed = summed + czr[4 * s + p]
+        car[p] = summed
     br[seq] = bs[seq]
     recv(br.at[pl.ds(0, 63)], 0)
     arrived = br[...].reshape(1024, 2 * HD)
@@ -340,16 +362,23 @@
     sent(azr.at[pl.ds(0, 15)], 3)
     sent(azmr.at[pl.ds(0, 15)], 4)
     sent(fox.at[pl.ds(0, 3)], 5)
-    sent(ybr.at[pl.ds(0, 7)], 6)
+    sent(ybr.at[pl.ds(0, 31)], 6)
+    sent(owx.at[pl.ds(0, 3)], 9)
     sent(cxr.at[pl.ds(0, 3)], 7)
-    sent(czr.at[pl.ds(0, 15)], 8)
-    sent(car.at[pl.ds(0, 3)], 9)
+    sent(czr.at[pl.ds(0, 63)], 8)
     sent(dxr.at[pl.ds(0, 3)], 10)
     compact_out.wait()
     recv(fin.at[pl.ds(0, 15)], 11)
     for h in range(HEADS):
         so_o[:, h * HD : (h + 1) * HD] = fin[:, h, :].astype(BF16)
     sent(fin.at[pl.ds(0, 15)], 11)
+
+
+def settle(a, b, c, d, a_o, b_o, c_o, d_o):
+    a_o[...] = a[...]
+    b_o[...] = b[...]
+    c_o[...] = c[...]
+    d_o[...] = d[...]
 
 
 def per_device(
@@ -362,7 +391,7 @@
     vmem = pl.BlockSpec(memory_space=pltpu.VMEM)
     smem = pl.BlockSpec(memory_space=pltpu.SMEM)
     v = pltpu.VMEM
-    return pl.pallas_call(
+    results = pl.pallas_call(
         step,
         out_shape=(
             jax.ShapeDtypeStruct((REQS, HEADS * HD), BF16),
@@ -374,17 +403,17 @@
         out_specs=(vmem, vmem, hbm, vmem),
         scratch_shapes=[
             v((REQS, HD), BF16), v((REQS, HEADS * HD), BF16), v((REQS, 2 * HD), BF16),
-            v((REQS, ROWS, 2 * HD), BF16), v((HEADS * HD, HD), BF16), v((1, HD), F32), v((HD, 10 * HD), BF16),
+            v((REQS, ROWS, 2 * HD), BF16), v((4, 2 * HD, HD), BF16), v((1, HD), F32), v((HD, 10 * HD), BF16),
             v((REQS, ROWS, 2 * HD), BF16), v((REQS, SEL), jnp.int32), v((1, HD), F32),
             v((4, 32, HD), BF16), v((64, 16, 2 * HD), BF16), v((64, 16, 2 * HD), BF16),
             v((512, 1024), BF16), v((512, 2 * HD), BF16),
             v((4, 32, HD), BF16), v((4, 1, HD), F32), v((4, 32, HD), BF16), v((4, 1, HD), F32),
             v((32, HD), BF16), v((1, HD), F32), v((16, 32, HD), BF16), v((16, 1, HD), F32),
             v((32, HD), BF16), v((4, 32, HD), BF16),
-            v((REQS, HD), F32), v((8, REQS, HD), F32),
+            v((4, REQS, HD), YT), v((32, REQS, HD), YT),
             v((4, 3, REQS, HD), F32), v((4, 3, REQS, HD), F32),
-            v((3, REQS, 1, HD), F32), v((16, 3, 1, HD), F32),
-            v((3, 1, HD), F32), v((4, 3, 1, HD), F32),
+            v((3, REQS, 1, HD), F32), v((64, 3, 1, HD), F32),
+            v((4, 3, 1, HD), F32),
             v((16, HD), F32), v((4, 16, HD), F32),
             v((8, HD), F32), v((16, 8, HD), F32),
             pltpu.SemaphoreType.DMA((10,)), pltpu.SemaphoreType.DMA((12,)), pltpu.SemaphoreType.DMA((12,)),
@@ -398,6 +427,13 @@
         hidden, filter_query, new_entry, filter_cache, out_weight, next_gain.reshape(1, -1),
         next_weight.reshape(next_weight.shape[0], -1), next_cache, lengths, selected, inverse,
     )
+    return pl.pallas_call(
+        settle,
+        out_shape=tuple(jax.ShapeDtypeStruct(o.shape, o.dtype) for o in results),
+        in_specs=[vmem] * 4,
+        out_specs=(vmem,) * 4,
+        name="settle",
+    )(*results)
 
 
 def solution(mesh):

time: 80.5 us -> 71.2 us (0.88)
  the two profiles are of different devices: /device:TPU:2 before, /device:TPU:8 now
where the time goes in v2:
time: 71.2 us; the launch traced here: 71 us
  Pallas kernels  70.4 us (99%)
    pallas_call x1, Pallas kernels, per_device(): pl.pallas_call(step, out_shape=(jax.ShapeDtypeStruct((REQS, HEADS * HD),...  68.7 us
    pallas_call x1, Pallas kernels, per_device(): pl.pallas_call(settle, out_shape=tuple((jax.ShapeDtypeStruct(o.shape, o.d...  1.7 us

profile of v2, /device:TPU:8, one launch (start us, length us, event | category | flops | bytes accessed | tf_op | source)
XLA Modules:
  0.0 71.0 jit_solution(17588296967299458839)
XLA Ops:
  0.6 68.7 %decode_step.1 = (bf16[16,1024]{1,0:T(8,128)(2,1)}, bf16[16,128]{1,0:T(8,128)(2,1)}, bf16[1,512,256]{2,1,0:T(8,128)(2,1)}, bf16[16,1024]{1,0:T(8,128)(2,1)}) custom-call(bf16[16,128]{1,0:T(8,128)(2,1)} %hidden_h.1, bf16[16,1024]{1,0:T(8,128)(2,1)} %fq_h.1, bf16[16,256]{1,0:T(8,128)(2,1)} %ne_h.1, bf16[16,128,256]{2,1,0:T(8,128)(2,1)} %fc_h.1, ...), custom_call_target="tpu_custom_call" | custom-call | tf_op jit(solution)/shard_map/decode_step/pallas_call | solution.py:394
  69.3 1.7 %settle.1 = (bf16[16,1024]{1,0:T(8,128)(2,1)}, bf16[16,128]{1,0:T(8,128)(2,1)}, bf16[1,512,256]{2,1,0:T(8,128)(2,1)}, bf16[16,1024]{1,0:T(8,128)(2,1)}) custom-call(bf16[16,1024]{1,0:T(8,128)(2,1)} %get-tuple-element.8.a, bf16[16,128]{1,0:T(8,128)(2,1)} %get-tuple-element.9.b, bf16[1,512,256]{2,1,0:T(8,128)(2,1)} %get-tuple-element.10.c, ...), custom_call_target="tpu_custom_call" | custom-call | tf_op jit(solution)/shard_map/settle/pallas_call | solution.py:430
